TPU v7x, 256 devices: a whole 4x4x8 slice. The times are simulated.
256 devices in a mesh: date: 4 (over x), prod: 64 (over z, y, core).
Axes of the slice: x: 4, y: 4, z: 8, core: 2. Of those that a mesh axis runs over, the one named last changes fastest.
Arguments:
- cash_codes: int32 [524288, 128], P('prod'), may hold values from -127 to 127
- block_scales: float32 [524288, 4], P('prod'), may hold values from 8.286408e-05 to 0.00082864077
- trade_kind: int32 [524288], P('prod'), may hold values 0 or 1
- strike: float32 [524288], P('prod'), may hold values from -0.1875 to 0.1875
- set_of_trade: int32 [524288], P('prod'), may hold values from 0 to 2047
- discount: bfloat16 [16, 128, 64], P('date'), may hold values from 0.29882812 to 1
- lag_dates: int32 [2048], P('prod'), may hold values from 1 to 2, as said below
- threshold: float32 [2048], P('prod'), may hold values from 0.3 to 3
Outputs:
- exposure: float32 [16, 2048, 64], P('date', 'prod')
Inputs may be any that keep to these rules, and one draw needn't show every extreme that they name: `lag_dates`: every draw holds some set with a margin period of 2 dates.
All inputs are finite; a program needn't handle non-finite values. No bound on the sum of `trade_kind` on one device may be relied on, other than what follows from the above.
Results may differ from a plain program's by a relative error of at most 0.0023.
Values sent between devices are 32-bit elements; how exact they have to be, the bound alone decides.
A program may use at most 64 MiB of HBM per device.

v0:
```python
import jax
import jax.numpy as jnp
from jax import lax
from jax.sharding import PartitionSpec as P

LAGMAX = 2


def passed_along(array, axis, by):
    peers = lax.axis_size(axis)
    pairs = [(i, i + by) for i in range(peers) if 0 <= i + by < peers]
    return lax.ppermute(array, axis, pairs)


def set_blocks(count, compute):
    block_size = 256
    block_total = count // block_size
    starts = block_size * jnp.arange(block_total, dtype=jnp.int32)
    results = lax.map(lambda first: compute(first, block_size), starts)
    return results


def on_device(
    cash_codes, block_scales, trade_kind, strike, set_of_trade, discount, lag_dates, threshold
):
    trade_rows, bucket_count = cash_codes.shape
    scale_count = block_scales.shape[1]
    cashflow = (
        cash_codes.astype(jnp.float32)
        * jnp.repeat(block_scales, bucket_count // scale_count, axis=1)
    ).astype(jnp.bfloat16)
    date_count = discount.shape[0]
    path_count = discount.shape[2]
    total_dates = date_count * lax.axis_size("date")
    date_index = lax.axis_index("date") * date_count + jnp.arange(date_count, dtype=jnp.int32)
    buckets = jnp.arange(bucket_count, dtype=jnp.int32)
    alive = buckets[None, :] >= date_index[:, None] * (bucket_count // total_dates)
    live = jnp.where(alive[:, :, None], discount, jnp.zeros_like(discount))
    raw_value = jnp.einsum("nk,dkp->ndp", cashflow, live, preferred_element_type=jnp.float32)
    option = (trade_kind == 1)[:, None, None]
    trade_value = jnp.where(
        option, jnp.maximum(raw_value - strike[:, None, None], 0.0), raw_value
    ).astype(jnp.bfloat16)
    owned_sets = lag_dates.shape[0]
    flattened = trade_value.reshape(trade_rows, date_count * path_count)

    def one_block(first, block_size):
        labels = first + jnp.arange(block_size, dtype=jnp.int32)
        member = (labels[:, None] == set_of_trade[None, :]).astype(jnp.bfloat16)
        return jnp.dot(member, flattened, preferred_element_type=jnp.float32)

    blocks = set_blocks(owned_sets * lax.axis_size("prod"), one_block)
    netted = lax.psum_scatter(
        blocks.reshape(owned_sets * lax.axis_size("prod"), date_count * path_count),
        "prod",
        scatter_dimension=0,
        tiled=True,
    )
    set_value = netted.reshape(owned_sets, date_count, path_count).transpose(1, 0, 2)
    previous = passed_along(set_value, "date", 1)
    extended = jnp.concatenate([previous, set_value], axis=0)
    lagged = jnp.zeros_like(set_value)
    for lag_step in range(1, LAGMAX + 1):
        chosen = (lag_dates == lag_step).astype(jnp.float32)[None, :, None]
        lagged = (
            lagged + chosen * extended[date_count - lag_step : date_count - lag_step + date_count]
        )
    limit = threshold[None, :, None]
    collateral = jnp.maximum(lagged - limit, 0.0) - jnp.maximum(-lagged - limit, 0.0)
    return jnp.maximum(set_value - collateral, 0.0)


def solution(mesh):
    placed = (
        P("prod", None),
        P("prod", None),
        P("prod"),
        P("prod"),
        P("prod"),
        P("date", None, None),
        P("prod"),
        P("prod"),
    )
    return jax.shard_map(
        on_device, mesh=mesh, in_specs=placed, out_specs=P("date", "prod", None), check_vma=False
    )
```

profile of v0, /device:TPU:102, one launch (start us, length us, event | category | flops | bytes accessed | tf_op | source)
XLA Modules:
  0.0 226.1 jit_solution(9118733644613281505)
XLA Ops:
  6.5 0.0 reduce-scatter.2.cloned.1.call-start
  6.5 0.0 copy-start.3
  6.5 0.0 copy-start
  6.6 5.6 %copy.15 = s32[8192,128]{0,1:T(8,128)} copy(s32[8192,128]{1,0:T(8,128)} %param.10) | data formatting | bytes 8388608 | tf_op args[0]
  12.2 0.1 iota_compare_fusion
  12.3 0.0 copy-done.3
  12.3 0.0 copy-done
  12.3 2.6 %fusion.10 = bf16[8192,128]{0,1:T(8,128)(2,1)S(1)} fusion(s32[8192,128]{0,1:T(8,128)} %copy.15, f32[8192,4]{0,1:T(4,128)S(1)} %copy-done), kind=kLoop, calls=%fused_computation.9 | loop fusion | flops 3145728 | bytes 6422528 | tf_op jit(solution)/shard_map/convert_element_type | solution.py:31
  14.9 0.0 copy-done.1
  15.0 0.0 copy-start.2
  15.0 1.2 fusion.15
  16.2 0.0 copy-done.2
  16.2 3.1 %select_convert_fusion = bf16[8192,4,64]{0,2,1:T(8,128)(2,1)} fusion(f32[8192,4,64]{0,2,1:T(8,128)S(1)} %bitcast.27, f32[8192]{0:T(1024)S(1)} %copy-done.2, pred[8192]{0:T(1024)(128)(4,1)S(1)} %broadcast_compare_fusion), kind=kLoop, calls=%fused_computation.7 | loop fusion | flops 8388608 | bytes 12623872 | tf_op jit(solution)/shard_map/convert_element_type | solution.py:43
  19.4 6.4 %copy.17 = bf16[8192,256]{1,0:T(8,128)(2,1)} copy(bf16[8192,256]{0,1:T(8,128)(2,1)} %bitcast.28) | data formatting | bytes 8388608 | tf_op jit(solution)/shard_map/while | solution.py:19
  25.7 0.0 copy-done.5
  25.7 44.3 %while.10 = (s32[]{:T(128)}, f32[8,256,256]{2,1,0:T(8,128)}, s32[8]{0:T(128)S(1)}, s32[8192]{0:T(1024)S(1)}, bf16[8192,256]{1,0:T(8,128)(2,1)}, /*index=5*/s32[]{:T(128)}) while((s32[]{:T(128)}, f32[8,256,256]{2,1,0:T(8,128)}, s32[8]{0:T(128)S(1)}, s32[8192]{0:T(1024)S(1)}, bf16[8192,256]{1,0:T(8,128)(2,1)}, /*index=5*/s32[]{:T(128)}) %tuple.27), condition=%wide.region_1.2_spmd, body=%wide.region_0.1_spmd.sunk | while | flops 1075839232 | bytes 4491861 | solution.py:19
  25.8 0.7 dynamic_slice.5
  26.4 0.7 iota_add_fusion.2
  27.1 4.2 %fusion.24 = f32[8,256,256]{2,1,0:T(8,128)} fusion(f32[8,256,256]{2,1,0:T(8,128)} %get-tuple-element.98, s32[]{:T(128)} %get-tuple-element.97, bf16[8192,256]{1,0:T(8,128)(2,1)} %get-tuple-element.107, s32[8192]{0:T(1024)S(1)} %get-tuple-element.106, s32[256]{0:T(256)S(1)} %iota_add_fusion.2), kind=kOutput, calls=%fused_computation.5.clone.1 | convolution fusion | flops 1075838976 | bytes 4490752 | tf_op jit(solution)/shard_map/while/body/eval_jaxpr/dot_general | solution.py:50
  31.3 0.6 dynamic_slice.5
  32.0 0.7 iota_add_fusion.2
  32.7 4.2 %fusion.24 = f32[8,256,256]{2,1,0:T(8,128)} fusion(f32[8,256,256]{2,1,0:T(8,128)} %get-tuple-element.98, s32[]{:T(128)} %get-tuple-element.97, bf16[8192,256]{1,0:T(8,128)(2,1)} %get-tuple-element.107, s32[8192]{0:T(1024)S(1)} %get-tuple-element.106, s32[256]{0:T(256)S(1)} %iota_add_fusion.2), kind=kOutput, calls=%fused_computation.5.clone.1 | convolution fusion | flops 1075838976 | bytes 4490752 | tf_op jit(solution)/shard_map/while/body/eval_jaxpr/dot_general | solution.py:50
  36.9 0.6 dynamic_slice.5
  37.5 0.7 iota_add_fusion.2
  38.2 4.2 %fusion.24 = f32[8,256,256]{2,1,0:T(8,128)} fusion(f32[8,256,256]{2,1,0:T(8,128)} %get-tuple-element.98, s32[]{:T(128)} %get-tuple-element.97, bf16[8192,256]{1,0:T(8,128)(2,1)} %get-tuple-element.107, s32[8192]{0:T(1024)S(1)} %get-tuple-element.106, s32[256]{0:T(256)S(1)} %iota_add_fusion.2), kind=kOutput, calls=%fused_computation.5.clone.1 | convolution fusion | flops 1075838976 | bytes 4490752 | tf_op jit(solution)/shard_map/while/body/eval_jaxpr/dot_general | solution.py:50
  42.4 0.6 dynamic_slice.5
  43.1 0.7 iota_add_fusion.2
  43.7 4.2 %fusion.24 = f32[8,256,256]{2,1,0:T(8,128)} fusion(f32[8,256,256]{2,1,0:T(8,128)} %get-tuple-element.98, s32[]{:T(128)} %get-tuple-element.97, bf16[8192,256]{1,0:T(8,128)(2,1)} %get-tuple-element.107, s32[8192]{0:T(1024)S(1)} %get-tuple-element.106, s32[256]{0:T(256)S(1)} %iota_add_fusion.2), kind=kOutput, calls=%fused_computation.5.clone.1 | convolution fusion | flops 1075838976 | bytes 4490752 | tf_op jit(solution)/shard_map/while/body/eval_jaxpr/dot_general | solution.py:50
  47.9 0.6 dynamic_slice.5
  48.6 0.7 iota_add_fusion.2
  49.3 4.2 %fusion.24 = f32[8,256,256]{2,1,0:T(8,128)} fusion(f32[8,256,256]{2,1,0:T(8,128)} %get-tuple-element.98, s32[]{:T(128)} %get-tuple-element.97, bf16[8192,256]{1,0:T(8,128)(2,1)} %get-tuple-element.107, s32[8192]{0:T(1024)S(1)} %get-tuple-element.106, s32[256]{0:T(256)S(1)} %iota_add_fusion.2), kind=kOutput, calls=%fused_computation.5.clone.1 | convolution fusion | flops 1075838976 | bytes 4490752 | tf_op jit(solution)/shard_map/while/body/eval_jaxpr/dot_general | solution.py:50
  53.5 0.6 dynamic_slice.5
  54.1 0.7 iota_add_fusion.2
  54.8 4.2 %fusion.24 = f32[8,256,256]{2,1,0:T(8,128)} fusion(f32[8,256,256]{2,1,0:T(8,128)} %get-tuple-element.98, s32[]{:T(128)} %get-tuple-element.97, bf16[8192,256]{1,0:T(8,128)(2,1)} %get-tuple-element.107, s32[8192]{0:T(1024)S(1)} %get-tuple-element.106, s32[256]{0:T(256)S(1)} %iota_add_fusion.2), kind=kOutput, calls=%fused_computation.5.clone.1 | convolution fusion | flops 1075838976 | bytes 4490752 | tf_op jit(solution)/shard_map/while/body/eval_jaxpr/dot_general | solution.py:50
  59.0 0.6 dynamic_slice.5
  59.6 0.7 iota_add_fusion.2
  60.3 4.2 %fusion.24 = f32[8,256,256]{2,1,0:T(8,128)} fusion(f32[8,256,256]{2,1,0:T(8,128)} %get-tuple-element.98, s32[]{:T(128)} %get-tuple-element.97, bf16[8192,256]{1,0:T(8,128)(2,1)} %get-tuple-element.107, s32[8192]{0:T(1024)S(1)} %get-tuple-element.106, s32[256]{0:T(256)S(1)} %iota_add_fusion.2), kind=kOutput, calls=%fused_computation.5.clone.1 | convolution fusion | flops 1075838976 | bytes 4490752 | tf_op jit(solution)/shard_map/while/body/eval_jaxpr/dot_general | solution.py:50
  64.5 0.6 dynamic_slice.5
  65.1 0.7 iota_add_fusion.2
  65.8 4.2 %fusion.24 = f32[8,256,256]{2,1,0:T(8,128)} fusion(f32[8,256,256]{2,1,0:T(8,128)} %get-tuple-element.98, s32[]{:T(128)} %get-tuple-element.97, bf16[8192,256]{1,0:T(8,128)(2,1)} %get-tuple-element.107, s32[8192]{0:T(1024)S(1)} %get-tuple-element.106, s32[256]{0:T(256)S(1)} %iota_add_fusion.2), kind=kOutput, calls=%fused_computation.5.clone.1 | convolution fusion | flops 1075838976 | bytes 4490752 | tf_op jit(solution)/shard_map/while/body/eval_jaxpr/dot_general | solution.py:50
  70.0 0.0 reduce-scatter.2.cloned.1.call-update
  70.1 141.4 %reduce-scatter.2.cloned.1.call-done = f32[32,256]{1,0:T(8,128)} async-done(((f32[2048,256]{1,0:T(8,128)}), f32[32,256]{1,0:T(8,128)}) %reduce-scatter.2.cloned.1.call-update) | async-done | bytes 32784 | tf_op jit(solution)/shard_map/reduce_scatter | solution.py:53
  211.5 0.8 reshape.51
  212.4 1.3 collective-permute-start
  213.7 0.0 copy-done.6
  213.7 4.8 %collective-permute-done = f32[4,32,64]{2,1,0:T(8,128)S(1)} collective-permute-done((f32[4,32,64]{2,1,0:T(8,128)S(1)}, f32[4,32,64]{2,1,0:T(8,128)S(1)}, u32[]{:S(2)}, u32[]{:S(2)}) %collective-permute-start) | collective-permute-done | bytes 32800 | tf_op jit(solution)/shard_map/ppermute | solution.py:12
  218.5 0.0 copy-done.4
  218.5 0.7 subtract_maximum_fusion
  (11 shorter events, 0.0 us)
Async XLA Ops:
  6.5 205.0 %reduce-scatter.2.cloned.1.call-start = ((), (), s32[]{:S(2)}) async-start(), calls=%async_computation.1 | async-start | bytes 2129920 | tf_op jit(solution)/shard_map/reduce_scatter | solution.py:53
  6.5 5.7 %copy-start.3 = (s32[8192]{0:T(1024)S(1)}, s32[8192]{0:T(1024)}, u32[]{:S(2)}) copy-start(s32[8192]{0:T(1024)} %param.12) | copy-start | bytes 98308
  6.5 5.8 %copy-start = (f32[8192,4]{0,1:T(4,128)S(1)}, f32[8192,4]{0,1:T(4,128)}, u32[]{:S(2)}) copy-start(f32[8192,4]{0,1:T(4,128)} %param.11) | copy-start | bytes 393220
  12.2 2.7 %copy-start.1 = (bf16[4,128,64]{1,2,0:T(8,128)(2,1)S(1)}, bf16[4,128,64]{1,2,0:T(8,128)(2,1)}, u32[]{:S(2)}) copy-start(bf16[4,128,64]{1,2,0:T(8,128)(2,1)} %param.15) | copy-start | bytes 196612
  15.0 1.3 copy-start.2
  19.4 6.4 %copy-start.5 = (s32[8192]{0:T(1024)S(1)}, s32[8192]{0:T(1024)}, u32[]{:S(2)}) copy-start(s32[8192]{0:T(1024)} %param.14) | copy-start | bytes 98308
  25.7 187.9 %copy-start.6 = (s32[32]{0:T(128)S(1)}, s32[32]{0:T(128)}, u32[]{:S(2)}) copy-start(s32[32]{0:T(128)} %param.16) | copy-start | bytes 388
  25.7 192.8 %copy-start.4 = (f32[32]{0:T(128)S(1)}, f32[32]{0:T(128)}, u32[]{:S(2)}) copy-start(f32[32]{0:T(128)} %param.17) | copy-start | bytes 388
  212.4 6.2 %collective-permute-start = (f32[4,32,64]{2,1,0:T(8,128)S(1)}, f32[4,32,64]{2,1,0:T(8,128)S(1)}, u32[]{:S(2)}, u32[]{:S(2)}) collective-permute-start(f32[4,32,64]{2,1,0:T(8,128)S(1)} %bitcast.31), channel_id=1, source_target_pairs={{0,64},{64,128},{128,192},{1,65},{65,129},{129,193},{2,66},{66,130... | collective-permute-start | bytes 98312 | tf_op jit(solution)/shard_map/ppermute | solution.py:12
Sparse Core Ops, SparseCore 0:
  70.2 141.2 reduce-scatter.1
where the time goes:
time: 229 us; the launch traced here: 226 us
  waiting for transfers between devices  146 us (64%)
  matrix products  34.9 us (15%)
  local copies, waits for them, and re-layouts  18.1 us (8%)
  between operations  13.5 us (6%)
  other arithmetic  12 us (5%)
    reduce_scatter x1, waiting for transfers between devices, on_device(): lax.psum_scatter(blocks.reshape(owned_sets * lax.axis_size('prod'), date_...  141 us
    dot_general x8, matrix products, one_block(): return jnp.dot(member, flattened, preferred_element_type=jnp.float32)  33.7 us
    while x1, local copies, waits for them, and re-layouts, set_blocks(): results = lax.map(lambda first: compute(first, block_size), starts)  6.37 us
    unnamed x15, local copies, waits for them, and re-layouts  5.67 us
    add x8, other arithmetic, one_block(): labels = first + jnp.arange(block_size, dtype=jnp.int32)  5.39 us
    dynamic_slice x8, local copies, waits for them, and re-layouts, set_blocks(): results = lax.map(lambda first: compute(first, block_size), starts)  5.17 us
    ppermute x1, waiting for transfers between devices, passed_along(): return lax.ppermute(array, axis, pairs)  4.84 us
  transfers between devices with their start and end apart: 2, of which 2 were waited for; matrix products, arithmetic and copies ran while one was open for 0% of the time, Pallas kernels for 0%

commit v1 on v0

v1 whole, which is shorter than its diff:
```python
import jax
import jax.numpy as jnp
from jax import lax
from jax.experimental import pallas as pl
from jax.experimental.pallas import tpu as pltpu
from jax.sharding import PartitionSpec as P

MESH = pl.DeviceIdType.MESH
NT = (((1,), (1,)), ((), ()))
Z, Y, CORES = 8, 4, 2
OWN = 32
TILE = Y * CORES * OWN
CHUNK = 1024
F32, BF16 = jnp.float32, jnp.bfloat16


def place(z, y, core):
    return (z * Y + y) * CORES + core


def kernel(
    codes_hbm, scales_ref, kind_ref, strike_ref, set_ref, live_ref, lag_ref, limit_ref, out_ref,
    codes, values, acc, pair_in, y_in, z_out, z_in, lag_out, lag_in,
    codes_sem, pair_s, pair_r, y_s, y_r, z_s, z_r, lag_s, lag_r,
):
    trades, buckets = codes.shape
    dates, owned, paths = out_ref.shape
    columns = dates * paths
    x = lax.axis_index("date")
    me = lax.axis_index("prod")
    core = lax.rem(me, CORES)
    y = lax.rem(me // CORES, Y)
    z = me // (CORES * Y)
    sibling = place(z, y, 1 - core)
    x_next = lax.rem(x + 1, lax.axis_size("date"))

    loads = []
    for j in range(trades // CHUNK):
        rows = pl.ds(j * CHUNK, CHUNK)
        load = pltpu.make_async_copy(codes_hbm.at[rows], codes.at[rows], codes_sem.at[j])
        load.start()
        loads.append(load)

    barrier = pltpu.get_barrier_semaphore()
    peers = [sibling]
    peers += [place(z, lax.rem(y + j, Y), core) for j in range(1, Y)]
    peers += [place(lax.rem(z + j, Z), y, core) for j in range(1, Z)]
    for peer in peers:
        pl.semaphore_signal(barrier, inc=1, device_id={"prod": peer}, device_id_type=MESH)
    x_last = lax.rem(x + lax.axis_size("date") - 1, lax.axis_size("date"))
    pl.semaphore_signal(barrier, inc=1, device_id={"date": x_last}, device_id_type=MESH)

    total_dates = dates * lax.axis_size("date")
    bucket = lax.broadcasted_iota(jnp.int32, (columns, buckets), 1)
    date = x * dates + lax.broadcasted_iota(jnp.int32, (columns, buckets), 0) // paths
    live = jnp.where(
        bucket >= date * (buckets // total_dates), live_ref[...].astype(F32), 0.0
    ).astype(BF16)
    blocks = scales_ref.shape[0]
    for j in range(trades // CHUNK):
        rows = pl.ds(j * CHUNK, CHUNK)
        loads[j].wait()
        code = codes[rows, :].astype(F32).astype(BF16).T.astype(F32)
        scale = scales_ref[:, rows]
        scale = jnp.concatenate(
            [jnp.broadcast_to(scale[b : b + 1], (buckets // blocks, CHUNK)) for b in range(blocks)],
            axis=0,
        )
        raw = jnp.dot(live, (code * scale).astype(BF16), preferred_element_type=F32)
        floored = jnp.maximum(raw - strike_ref[:, rows], 0.0)
        values[:, rows] = jnp.where(kind_ref[:, rows] == 1, floored, raw).astype(BF16)

    r = lax.broadcasted_iota(jnp.int32, (TILE, 128), 0)
    block = r // OWN
    to_core = jnp.where(block < Y, core, 1 - core)
    label = (lax.rem(y + lax.rem(block, Y), Y) * CORES + to_core) * OWN + lax.rem(r, OWN)

    def tile_z(k):
        far = Z // 2 - (k + 1) // 2
        away = jnp.where(lax.rem(k, 2) == 1, far, Z - far)
        return lax.rem(z + away, Z)

    def pair_copy(k):
        return pltpu.make_async_remote_copy(
            src_ref=acc.at[k, pl.ds(TILE // 2, TILE // 2)], dst_ref=pair_in.at[k],
            send_sem=pair_s.at[k], recv_sem=pair_r.at[k],
            device_id={"prod": sibling}, device_id_type=MESH,
        )

    def y_copy(k, j):
        return pltpu.make_async_remote_copy(
            src_ref=acc.at[k, pl.ds(j * OWN, OWN)], dst_ref=y_in.at[k, j - 1],
            send_sem=y_s.at[k, j - 1], recv_sem=y_r.at[k, j - 1],
            device_id={"prod": place(z, lax.rem(y + j, Y), core)}, device_id_type=MESH,
        )

    def z_copy(k):
        return pltpu.make_async_remote_copy(
            src_ref=z_out.at[k], dst_ref=z_in.at[k], send_sem=z_s.at[k], recv_sem=z_r.at[k],
            device_id={"prod": place(tile_z(k), y, core)}, device_id_type=MESH,
        )

    def after_pair(k):
        pair_copy(k).wait_recv()
        acc[k, : TILE // 2] += pair_in[k]
        for j in (2, 1, 3):
            y_copy(k, j).start()

    def y_total(k):
        for j in range(1, Y):
            y_copy(k, j).wait_recv()
        return acc[k, :OWN] + y_in[k, 0] + y_in[k, 1] + y_in[k, 2]

    def after_y(k):
        z_out[k] = y_total(k)
        z_copy(k).start()

    sets16 = set_ref[...].astype(jnp.int16)

    def step(k, carry):
        wanted = (label + tile_z(k) * TILE).astype(jnp.int16)
        wanted = jnp.concatenate([wanted] * (trades // 128), axis=1)
        member = jnp.where(wanted == sets16, BF16(1), BF16(0))
        acc[k] = lax.dot_general(member, values[...], NT, preferred_element_type=F32)

        @pl.when(k == 0)
        def _():
            pl.semaphore_wait(barrier, len(peers) + 1)

        pair_copy(k).start()

        @pl.when(k >= 1)
        def _():
            after_pair(k - 1)

        @pl.when(k >= 4)
        def _():
            after_y(k - 4)

        return carry

    lax.fori_loop(0, Z, step, 0)
    after_pair(Z - 1)
    for k in range(Z - 4, Z - 1):
        after_y(k)
    total = y_total(Z - 1)
    for k in range(Z - 1):
        z_copy(k).wait_recv()
        total = total + z_in[k]

    half = columns // 2
    lag_out[...] = total[:, half:]
    lag_copy = pltpu.make_async_remote_copy(
        src_ref=lag_out, dst_ref=lag_in, send_sem=lag_s.at[0], recv_sem=lag_r.at[0],
        device_id={"date": x_next}, device_id_type=MESH,
    )
    lag_copy.start()
    diagonal = lax.broadcasted_iota(jnp.int32, (owned, owned), 0) == lax.broadcasted_iota(
        jnp.int32, (owned, owned), 1
    )
    lag = jnp.sum(jnp.where(diagonal, lag_ref[...].astype(F32), 0.0), axis=1, keepdims=True)
    limit = jnp.sum(jnp.where(diagonal, limit_ref[...], 0.0), axis=1, keepdims=True)
    lag_copy.wait_recv()
    previous = jnp.where(x > 0, lag_in[...], 0.0)
    lag_one = jnp.concatenate([previous[:, paths:], total[:, : 3 * paths]], axis=1)
    lag_two = jnp.concatenate([previous, total[:, : 2 * paths]], axis=1)
    lagged = jnp.where(lag == 1.0, lag_one, jnp.where(lag == 2.0, lag_two, 0.0))
    collateral = jnp.maximum(lagged - limit, 0.0) - jnp.maximum(-lagged - limit, 0.0)
    exposure = jnp.maximum(total - collateral, 0.0)
    for d in range(dates):
        out_ref[d] = exposure[:, d * paths : (d + 1) * paths]

    for k in range(Z):
        pair_copy(k).wait_send()
        for j in range(1, Y):
            y_copy(k, j).wait_send()
        if k < Z - 1:
            z_copy(k).wait_send()
    lag_copy.wait_send()


def on_device(cash_codes, block_scales, trade_kind, strike, set_of_trade, discount, lag, limit):
    trades, buckets = cash_codes.shape
    dates, _, paths = discount.shape
    columns = dates * paths
    owned = lag.shape[0]
    live = jnp.swapaxes(discount, 1, 2).reshape(columns, buckets)
    vmem = pl.BlockSpec(memory_space=pltpu.VMEM)
    dma = pltpu.SemaphoreType.DMA
    return pl.pallas_call(
        kernel,
        out_shape=jax.ShapeDtypeStruct((dates, owned, paths), F32),
        in_specs=[pl.BlockSpec(memory_space=pl.ANY)] + [vmem] * 7,
        out_specs=vmem,
        scratch_shapes=[
            pltpu.VMEM((trades, buckets), jnp.int32),
            pltpu.VMEM((columns, trades), BF16),
            pltpu.VMEM((Z, TILE, columns), F32),
            pltpu.VMEM((Z, TILE // 2, columns), F32),
            pltpu.VMEM((Z, Y - 1, OWN, columns), F32),
            pltpu.VMEM((Z - 1, OWN, columns), F32),
            pltpu.VMEM((Z - 1, OWN, columns), F32),
            pltpu.VMEM((OWN, columns // 2), F32),
            pltpu.VMEM((OWN, columns // 2), F32),
            dma((trades // CHUNK,)),
            dma((Z,)), dma((Z,)), dma((Z, Y - 1)), dma((Z, Y - 1)),
            dma((Z - 1,)), dma((Z - 1,)), dma((1,)), dma((1,)),
        ],
        compiler_params=pltpu.CompilerParams(
            collective_id=0, has_side_effects=True, vmem_limit_bytes=50 << 20
        ),
        name="exposure",
    )(
        cash_codes, block_scales.T, trade_kind[None], strike[None], set_of_trade[None], live,
        lag[None], limit[None],
    )


def solution(mesh):
    placed = (
        P("prod", None), P("prod", None), P("prod"), P("prod"), P("prod"),
        P("date", None, None), P("prod"), P("prod"),
    )
    return jax.shard_map(
        on_device, mesh=mesh, in_specs=placed, out_specs=P("date", "prod", None), check_vma=False
    )
```

time: 229 us -> 37.8 us (0.17)
  the two profiles are of different devices: /device:TPU:102 before, /device:TPU:96 now
where the time goes in v1:
time: 37.8 us; the launch traced here: 37.4 us
  Pallas kernels  31.4 us (83%)
  local copies, waits for them, and re-layouts  5.96 us (16%)
    pallas_call x1, Pallas kernels, on_device(): pl.pallas_call(kernel, out_shape=jax.ShapeDtypeStruct((dates, owned, path...  31.4 us
    unnamed x15, local copies, waits for them, and re-layouts  5.96 us

profile of v1, /device:TPU:96, one launch (start us, length us, event | category | flops | bytes accessed | tf_op | source)
XLA Modules:
  0.0 37.4 jit_solution(14339455936669829819)
XLA Ops:
  0.0 0.0 copy-start
  0.0 0.9 %copy-done = f32[8192,4]{0,1:T(4,128)S(1)} copy-done((f32[8192,4]{0,1:T(4,128)S(1)}, f32[8192,4]{0,1:T(4,128)}, u32[]{:S(2)}) %copy-start) | copy-done | bytes 131096
  0.9 0.0 copy-start.1
  0.9 0.8 %copy-done.1 = bf16[4,128,64]{1,2,0:T(8,128)(2,1)S(1)} copy-done((bf16[4,128,64]{1,2,0:T(8,128)(2,1)S(1)}, bf16[4,128,64]{1,2,0:T(8,128)(2,1)}, u32[]{:S(2)}) %copy-start.1) | copy-done | bytes 65560
  1.7 0.0 copy-start.2
  1.7 0.8 %copy-done.2 = s32[8192]{0:T(1024)S(1)} copy-done((s32[8192]{0:T(1024)S(1)}, s32[8192]{0:T(1024)}, u32[]{:S(2)}) %copy-start.2) | copy-done | bytes 32792
  2.5 0.0 copy-start.3
  2.5 0.8 %copy-done.3 = f32[8192]{0:T(1024)S(1)} copy-done((f32[8192]{0:T(1024)S(1)}, f32[8192]{0:T(1024)}, u32[]{:S(2)}) %copy-start.3) | copy-done | bytes 32792
  3.3 0.0 copy-start.4
  3.3 0.8 %copy-done.4 = s32[8192]{0:T(1024)S(1)} copy-done((s32[8192]{0:T(1024)S(1)}, s32[8192]{0:T(1024)}, u32[]{:S(2)}) %copy-start.4) | copy-done | bytes 32792
  4.0 0.0 copy-start.5
  4.0 0.7 %copy-done.5 = s32[32]{0:T(128)S(1)} copy-done((s32[32]{0:T(128)S(1)}, s32[32]{0:T(128)}, u32[]{:S(2)}) %copy-start.5) | copy-done | bytes 152
  4.7 0.0 copy-start.6
  4.7 0.7 %copy-done.6 = f32[32]{0:T(128)S(1)} copy-done((f32[32]{0:T(128)S(1)}, f32[32]{0:T(128)}, u32[]{:S(2)}) %copy-start.6) | copy-done | bytes 152
  5.3 31.4 %exposure.1 = f32[4,32,64]{2,1,0:T(8,128)S(1)} custom-call(s32[8192,128]{1,0:T(8,128)} %codes_hbm.1, f32[4,8192]{1,0:T(4,128)S(1)} %bitcast.9, s32[1,8192]{1,0:T(1,128)S(1)} %bitcast.11, f32[1,8192]{1,0:T(1,128)S(1)} %bitcast.12, s32[1,8192]{1,0:T(1,128)S(1)} %bitcast.13, bf16[256,128]{1,0:T(8,128)(2,1)S(1)} %bitcast.10, s32[1,32]{1,0:T(1,128)S(1)} %bitcast.14, ...), custom_call_target="tpu_custom_call" | custom-call | tf_op jit(solution)/shard_map/exposure/pallas_call | solution.py:190
  36.8 0.6 %copy.10 = f32[4,32,64]{2,1,0:T(8,128)} copy(f32[4,32,64]{2,1,0:T(8,128)S(1)} %exposure.1) | data formatting | bytes 65536
Async XLA Ops:
  0.0 0.9 %copy-start = (f32[8192,4]{0,1:T(4,128)S(1)}, f32[8192,4]{0,1:T(4,128)}, u32[]{:S(2)}) copy-start(f32[8192,4]{0,1:T(4,128)} %param.9) | copy-start | bytes 393220
  0.9 0.8 %copy-start.1 = (bf16[4,128,64]{1,2,0:T(8,128)(2,1)S(1)}, bf16[4,128,64]{1,2,0:T(8,128)(2,1)}, u32[]{:S(2)}) copy-start(bf16[4,128,64]{1,2,0:T(8,128)(2,1)} %param.13) | copy-start | bytes 196612
  1.7 0.8 %copy-start.2 = (s32[8192]{0:T(1024)S(1)}, s32[8192]{0:T(1024)}, u32[]{:S(2)}) copy-start(s32[8192]{0:T(1024)} %param.10) | copy-start | bytes 98308
  2.5 0.8 %copy-start.3 = (f32[8192]{0:T(1024)S(1)}, f32[8192]{0:T(1024)}, u32[]{:S(2)}) copy-start(f32[8192]{0:T(1024)} %param.11) | copy-start | bytes 98308
  3.3 0.8 %copy-start.4 = (s32[8192]{0:T(1024)S(1)}, s32[8192]{0:T(1024)}, u32[]{:S(2)}) copy-start(s32[8192]{0:T(1024)} %param.12) | copy-start | bytes 98308
  4.0 0.7 %copy-start.5 = (s32[32]{0:T(128)S(1)}, s32[32]{0:T(128)}, u32[]{:S(2)}) copy-start(s32[32]{0:T(128)} %param.14) | copy-start | bytes 388
  4.7 0.7 %copy-start.6 = (f32[32]{0:T(128)S(1)}, f32[32]{0:T(128)}, u32[]{:S(2)}) copy-start(f32[32]{0:T(128)} %param.15) | copy-start | bytes 388

commit v2 on v1

v2 whole, which is shorter than its diff:
```python
import jax
import jax.numpy as jnp
from jax import lax
from jax.experimental import pallas as pl
from jax.experimental.pallas import tpu as pltpu
from jax.sharding import PartitionSpec as P

MESH = pl.DeviceIdType.MESH
NT = (((1,), (1,)), ((), ()))
Z, Y, CORES = 8, 4, 2
OWN = 32
CELLS = 4
TILE = CELLS * CORES * OWN
WHOLE = 4
CHUNK = 2048
Y_LAG = 5
EARLY = 2
F32, BF16 = jnp.float32, jnp.bfloat16


def place(z, y, core):
    return (z * Y + y) * CORES + core


def kernel(
    codes_hbm, scales_hbm, kind_hbm, strike_hbm, set_hbm, live_hbm, lag_hbm, limit_hbm, out_ref,
    codes, scales_ref, kind_ref, strike_ref, set_ref, live_ref, lag_ref, limit_ref,
    values, acc, pair_in, y_in, z_out, z_in, lag_out, lag_in,
    codes_sem, small_sem, pair_s, pair_r, y_s, y_r, z_s, z_r, lag_s, lag_r,
):
    trades, buckets = codes.shape
    dates, owned, paths = out_ref.shape
    columns = dates * paths
    half = columns // 2
    x = lax.axis_index("date")
    me = lax.axis_index("prod")
    core = lax.rem(me, CORES)
    y = lax.rem(me // CORES, Y)
    z = me // (CORES * Y)
    sibling = place(z, y, 1 - core)
    x_size = lax.axis_size("date")
    x_next = lax.rem(x + 1, x_size)

    small = []
    for i, (src, dst) in enumerate((
        (live_hbm, live_ref), (scales_hbm, scales_ref), (strike_hbm, strike_ref), (kind_hbm, kind_ref),
        (set_hbm, set_ref), (lag_hbm, lag_ref), (limit_hbm, limit_ref),
    )):
        small.append(pltpu.make_async_copy(src, dst, small_sem.at[i]))
    loads = []
    for j in range(trades // CHUNK):
        rows = pl.ds(j * CHUNK, CHUNK)
        loads.append(pltpu.make_async_copy(codes_hbm.at[rows], codes.at[rows], codes_sem.at[j]))
    loads[0].start()
    for load in small:
        load.start()
    for load in loads[1:]:
        load.start()

    barrier = pltpu.get_barrier_semaphore()
    near = [place(z, lax.rem(y + j, Y), core) for j in range(1, Y)]
    near += [place(lax.rem(z + j, Z), y, core) for j in range(1, Z)]
    for peer in [sibling] + near:
        pl.semaphore_signal(barrier, inc=1, device_id={"prod": peer}, device_id_type=MESH)

    @pl.when(x > 0)
    def _():
        pl.semaphore_signal(barrier, inc=1, device_id={"date": x - 1}, device_id_type=MESH)

    for load in small[:4]:
        load.wait()
    total_dates = dates * x_size
    bucket = lax.broadcasted_iota(jnp.int32, (columns, buckets), 1)
    date = x * dates + lax.broadcasted_iota(jnp.int32, (columns, buckets), 0) // paths
    live = jnp.where(
        bucket >= date * (buckets // total_dates), live_ref[...].astype(F32), 0.0
    ).astype(BF16)
    blocks = scales_ref.shape[0]

    def z_of(i):
        plain = jnp.where(i < z, i, i + 1)
        plain = jnp.where((z == 4) & (i >= 4), 11 - i, plain)
        plain = jnp.where((z == 5) & (i >= 5), 12 - i, plain)
        return jnp.where(i == Z - 1, z, plain)

    def cell(k, i):
        n = jnp.maximum((k - WHOLE) * CELLS + i, 0)
        dy = jnp.where(k < WHOLE, i, jnp.where(k == Z - 1, 0, lax.rem(n, Y - 1) + 1))
        which = jnp.where(k < WHOLE, k, WHOLE + jnp.where(k == Z - 1, i, n // (Y - 1)))
        return dy, which

    own_row = lax.broadcasted_iota(jnp.int32, (OWN, 128), 0)

    def set_sums(k, first, count):
        bases = []
        for i in range(CELLS):
            dy, which = cell(k, i)
            bases.append(place(z_of(which), lax.rem(y + dy, Y), 0) * OWN)
        wanted = jnp.concatenate(
            [own_row + (base + to * OWN) for to in (core, 1 - core) for base in bases], axis=0
        ).astype(jnp.int16)
        wanted = jnp.concatenate([wanted] * (count // 128), axis=1)
        rows = pl.ds(first, count)
        sets = set_ref[:, rows].astype(jnp.int16)
        member = jnp.where(wanted == sets, BF16(1), BF16(0))
        return lax.dot_general(member, values[:, rows], NT, preferred_element_type=F32)

    def early_sums(k, j):
        part = set_sums(k, j * CHUNK, CHUNK)
        acc[k] = part if j == 0 else acc[k] + part

    for j in range(trades // CHUNK):
        rows = pl.ds(j * CHUNK, CHUNK)
        loads[j].wait()
        code = codes[rows, :].astype(F32).astype(BF16).T.astype(F32)
        scale = scales_ref[:, rows]
        scale = jnp.concatenate(
            [jnp.broadcast_to(scale[b : b + 1], (buckets // blocks, CHUNK)) for b in range(blocks)],
            axis=0,
        )
        raw = jnp.dot(live, (code * scale).astype(BF16), preferred_element_type=F32)
        floored = jnp.maximum(raw - strike_ref[:, rows], 0.0)
        values[:, rows] = jnp.where(kind_ref[:, rows] == 1, floored, raw).astype(BF16)
        if j == 0:
            for load in small[4:]:
                load.wait()
        else:
            for k in range(EARLY):
                early_sums(k, j - 1)

    def pair_copy(k):
        return pltpu.make_async_remote_copy(
            src_ref=acc.at[k, pl.ds(TILE // 2, TILE // 2)], dst_ref=pair_in.at[k],
            send_sem=pair_s.at[k], recv_sem=pair_r.at[k],
            device_id={"prod": sibling}, device_id_type=MESH,
        )

    def y_copy(k, i):
        dy, which = cell(k, i)
        return pltpu.make_async_remote_copy(
            src_ref=acc.at[k, pl.ds(i * OWN, OWN)], dst_ref=y_in.at[which, dy - 1],
            send_sem=y_s.at[which, dy - 1], recv_sem=y_r.at[which, dy - 1],
            device_id={"prod": place(z, lax.rem(y + dy, Y), core)}, device_id_type=MESH,
        )

    def y_arrival(which, j):
        return pltpu.make_async_remote_copy(
            src_ref=z_out.at[0], dst_ref=y_in.at[which, j],
            send_sem=y_s.at[which, j], recv_sem=y_r.at[which, j],
            device_id={"prod": me}, device_id_type=MESH,
        )

    def z_copy(which, source):
        return pltpu.make_async_remote_copy(
            src_ref=z_out.at[which], dst_ref=z_in.at[source],
            send_sem=z_s.at[which], recv_sem=z_r.at[source],
            device_id={"prod": place(z_of(which), y, core)}, device_id_type=MESH,
        )

    has_next = x < x_size - 1

    def after_pair(k):
        pair_copy(k).wait_recv()
        acc[k, : TILE // 2] += pair_in[k]

        @pl.when(k >= WHOLE)
        def _():
            y_copy(k, 0).start()

        for i in (2, 1, 3):
            y_copy(k, i).start()

    def y_total(which):
        for j in range(Y - 1):
            y_arrival(which, j).wait_recv()
        whole = isinstance(which, jax.Array) or which < WHOLE
        total = acc[which, :OWN] if whole else acc[Z - 1, (which - WHOLE) * OWN : (which - WHOLE + 1) * OWN]
        for j in range(Y - 1):
            total = total + y_in[which, j]
        return total

    def after_y(which):
        z_out[which] = y_total(which)
        z_copy(which, z).start()

    last = trades // CHUNK - 1
    for k in range(EARLY):
        early_sums(k, last)
        if k == 0:
            pl.semaphore_wait(barrier, len(near) + 1 + has_next.astype(jnp.int32))
        pair_copy(k).start()

    def step(k, carry):
        acc[k] = set_sums(k, 0, trades)
        pair_copy(k).start()

        @pl.when(k == EARLY)
        def _():
            for i in range(EARLY - 1):
                after_pair(i)

        after_pair(k - 1)

        @pl.when(k >= Y_LAG)
        def _():
            after_y(k - Y_LAG)

        return carry

    lax.fori_loop(EARLY, Z, step, 0)
    for which in range(Z - Y_LAG, WHOLE):
        after_y(which)
    pair_copy(Z - 1).wait_recv()
    acc[Z - 1, : TILE // 2] += pair_in[Z - 1]
    for which in range(WHOLE, Z - 1):
        after_y(which)
    diagonal = lax.broadcasted_iota(jnp.int32, (owned, owned), 0) == lax.broadcasted_iota(
        jnp.int32, (owned, owned), 1
    )
    lag = jnp.sum(jnp.where(diagonal, lag_ref[...].astype(F32), 0.0), axis=1, keepdims=True)
    limit = jnp.sum(jnp.where(diagonal, limit_ref[...], 0.0), axis=1, keepdims=True)
    for k in range(Z):
        pair_copy(k).wait_send()
        for j in range(Y - 1):
            y_arrival(k, j).wait_send()
        if k < Z - 1:
            z_copy(k, z).wait_send()
    total = y_total(Z - 1)
    for j in range(Z):
        pl.when(j != z)(z_copy(0, j).wait_recv)
    z_in[z] = jnp.zeros_like(total)
    for j in range(Z):
        total = total + z_in[j]

    lag_out[...] = total[:, half:]
    lag_copy = pltpu.make_async_remote_copy(
        src_ref=lag_out, dst_ref=lag_in, send_sem=lag_s.at[0], recv_sem=lag_r.at[0],
        device_id={"date": x_next}, device_id_type=MESH,
    )
    pl.when(has_next)(lag_copy.start)
    pl.when(x > 0)(lag_copy.wait_recv)
    previous = jnp.where(x > 0, lag_in[...], 0.0)
    lag_one = jnp.concatenate([previous[:, paths:], total[:, : 3 * paths]], axis=1)
    lag_two = jnp.concatenate([previous, total[:, : 2 * paths]], axis=1)
    lagged = jnp.where(lag == 1.0, lag_one, jnp.where(lag == 2.0, lag_two, 0.0))
    collateral = jnp.maximum(lagged - limit, 0.0) - jnp.maximum(-lagged - limit, 0.0)
    exposure = jnp.maximum(total - collateral, 0.0)
    for d in range(dates):
        out_ref[d] = exposure[:, d * paths : (d + 1) * paths]

    pl.when(has_next)(lag_copy.wait_send)


def on_device(cash_codes, block_scales, trade_kind, strike, set_of_trade, discount, lag, limit):
    trades, buckets = cash_codes.shape
    dates, _, paths = discount.shape
    columns = dates * paths
    owned = lag.shape[0]
    live = jnp.swapaxes(discount, 1, 2).reshape(columns, buckets)
    vmem, dma = pltpu.VMEM, pltpu.SemaphoreType.DMA
    operands = (
        cash_codes, block_scales.T, trade_kind[None], strike[None], set_of_trade[None], live,
        lag[None], limit[None],
    )
    return pl.pallas_call(
        kernel,
        out_shape=jax.ShapeDtypeStruct((dates, owned, paths), F32),
        in_specs=[pl.BlockSpec(memory_space=pl.ANY)] * len(operands),
        out_specs=pl.BlockSpec(memory_space=vmem),
        scratch_shapes=[vmem(operand.shape, operand.dtype) for operand in operands]
        + [
            vmem((columns, trades), BF16),
            vmem((Z, TILE, columns), F32),
            vmem((Z, TILE // 2, columns), F32),
            vmem((Z, Y - 1, OWN, columns), F32),
            vmem((Z - 1, OWN, columns), F32),
            vmem((Z, OWN, columns), F32),
            vmem((OWN, columns // 2), F32),
            vmem((OWN, columns // 2), F32),
            dma((trades // CHUNK,)), dma((len(operands) - 1,)),
            dma((Z,)), dma((Z,)), dma((Z, Y - 1)), dma((Z, Y - 1)),
            dma((Z,)), dma((Z,)), dma((1,)), dma((1,)),
        ],
        compiler_params=pltpu.CompilerParams(
            collective_id=0, has_side_effects=True, vmem_limit_bytes=63 << 20
        ),
        name="exposure",
    )(*operands)


def solution(mesh):
    placed = (
        P("prod", None), P("prod", None), P("prod"), P("prod"), P("prod"),
        P("date", None, None), P("prod"), P("prod"),
    )
    return jax.shard_map(
        on_device, mesh=mesh, in_specs=placed, out_specs=P("date", "prod", None), check_vma=False
    )
```

time: 37.8 us -> 31 us (0.82)
  the two profiles are of different devices: /device:TPU:96 before, /device:TPU:102 now
where the time goes in v2:
time: 31 us; the launch traced here: 30.6 us
  Pallas kernels  29.1 us (94%)
  local copies, waits for them, and re-layouts  1.47 us (5%)
    pallas_call x1, Pallas kernels, on_device(): pl.pallas_call(kernel, out_shape=jax.ShapeDtypeStruct((dates, owned, path...  29.1 us
    unnamed x1, local copies, waits for them, and re-layouts  1.47 us

profile of v2, /device:TPU:102, one launch (start us, length us, event | category | flops | bytes accessed | tf_op | source)
XLA Modules:
  0.0 30.6 jit_solution(8648943803123078524)
XLA Ops:
  0.0 29.1 %exposure.1 = f32[4,32,64]{2,1,0:T(8,128)} custom-call(s32[8192,128]{1,0:T(8,128)} %codes_hbm.1, f32[4,8192]{1,0:T(4,128)} %bitcast.9, s32[1,8192]{1,0:T(1,128)} %bitcast.11, f32[1,8192]{1,0:T(1,128)} %bitcast.12, s32[1,8192]{1,0:T(1,128)} %bitcast.13, bf16[256,128]{1,0:T(8,128)(2,1)} %bitcast.10, s32[1,32]{1,0:T(1,128)} %bitcast.14, f32[1,32]{1,0:T(1,128)} %bitcast.15), custom_call_target="tpu_custom_call" | custom-call | tf_op jit(solution)/shard_map/exposure/pallas_call | solution.py:265
  29.1 1.5 %copy.10 = f32[4,32,64]{2,1,0:T(8,128)} copy(f32[4,32,64]{2,1,0:T(8,128)} %exposure.1) | data formatting | bytes 65536

commit v3 on v2

v3 whole, which is shorter than its diff:
```python
import functools

import jax
import jax.numpy as jnp
from jax import lax
from jax.experimental import pallas as pl
from jax.experimental.pallas import tpu as pltpu
from jax.sharding import PartitionSpec as P

MESH = pl.DeviceIdType.MESH
NT = (((1,), (1,)), ((), ()))
Z, Y, CORES = 8, 4, 2
OWN = 32
CELLS = 4
TILE = CELLS * CORES * OWN
OWN_Z = 7
TILES = (
    ((0, 0), (1, 0), (2, 0), (3, 0)),
    ((0, 1), (1, 1), (2, 1), (3, 1)),
    ((0, 2), (1, 2), (2, 2), (3, 2)),
    ((0, 3), (1, 3), (2, 3), (3, 3)),
    ((1, 4), (2, 4), (3, 4), (1, 5)),
    ((2, 5), (3, 5), (1, 6), (2, 6)),
    ((3, 6), (1, 7), (2, 7), (3, 7)),
    ((0, 4), (0, 5), (0, 6), (0, 7)),
)
CHUNKS = (2048, 2048, 2048, 2048)
Y_LAG = 5
EARLY = 2
F32, BF16 = jnp.float32, jnp.bfloat16


def place(z, y, core):
    return (z * Y + y) * CORES + core


def kernel(
    codes_hbm, scales_hbm, kind_hbm, strike_hbm, set_hbm, live_hbm, lag_hbm, limit_hbm, out_ref,
    codes, scales_ref, kind_ref, strike_ref, set_ref, live_ref, lag_ref, limit_ref,
    values, wanted, acc, pair_in, y_in, z_out, z_in, lag_out, lag_in,
    codes_sem, small_sem, pair_s, pair_r, y_s, y_r, z_s, z_r, lag_s, lag_r,
):
    trades, buckets = codes.shape
    dates, owned, paths = out_ref.shape
    columns = dates * paths
    half = columns // 2
    x = lax.axis_index("date")
    me = lax.axis_index("prod")
    core = lax.rem(me, CORES)
    y = lax.rem(me // CORES, Y)
    z = me // (CORES * Y)
    sibling = place(z, y, 1 - core)
    x_size = lax.axis_size("date")
    x_next = lax.rem(x + 1, x_size)

    small = []
    for i, (src, dst) in enumerate((
        (live_hbm, live_ref), (scales_hbm, scales_ref), (strike_hbm, strike_ref), (kind_hbm, kind_ref),
        (set_hbm, set_ref), (lag_hbm, lag_ref), (limit_hbm, limit_ref),
    )):
        small.append(pltpu.make_async_copy(src, dst, small_sem.at[i]))
    loads = []
    pieces = [pl.ds(sum(CHUNKS[:j]), count) for j, count in enumerate(CHUNKS)]
    for j, rows in enumerate(pieces):
        loads.append(pltpu.make_async_copy(codes_hbm.at[rows], codes.at[rows], codes_sem.at[j]))
    loads[0].start()
    for load in small:
        load.start()
    for load in loads[1:]:
        load.start()

    barrier = pltpu.get_barrier_semaphore()
    near = [place(z, lax.rem(y + j, Y), core) for j in range(1, Y)]
    near += [place(lax.rem(z + j, Z), y, core) for j in range(1, Z)]
    for peer in [sibling] + near:
        pl.semaphore_signal(barrier, inc=1, device_id={"prod": peer}, device_id_type=MESH)

    @pl.when(x > 0)
    def _():
        pl.semaphore_signal(barrier, inc=1, device_id={"date": x - 1}, device_id_type=MESH)

    def z_of(i):
        plain = jnp.where(i < z, i, i + 1)
        plain = jnp.where((z == 4) & (i >= 4), 11 - i, plain)
        plain = jnp.where((z == 5) & (i >= 5), 12 - i, plain)
        return jnp.where(i == Z - 1, z, plain)

    planes = [z_of(jnp.int32(i)) for i in range(Z)]
    rows_y = [lax.rem(y + dy, Y) for dy in range(Y)]

    own_row = lax.broadcasted_iota(jnp.int32, (OWN, 128), 0)
    for k, tile in enumerate(TILES):
        for i, (dy, plane) in enumerate(tile):
            for half_tile, to in enumerate((core, 1 - core)):
                row = (half_tile * CELLS + i) * OWN
                wanted[k, row : row + OWN] = (
                    own_row + place(planes[plane], rows_y[dy], to) * OWN
                ).astype(jnp.int16)

    for load in small[:4]:
        load.wait()
    total_dates = dates * x_size
    bucket = lax.broadcasted_iota(jnp.int32, (columns, buckets), 1)
    date = x * dates + lax.broadcasted_iota(jnp.int32, (columns, buckets), 0) // paths
    live = jnp.where(
        bucket >= date * (buckets // total_dates), live_ref[...].astype(F32), 0.0
    ).astype(BF16)
    blocks = scales_ref.shape[0]

    def rows_of(cell):
        k = [n for n, tile in enumerate(TILES) if cell in tile][0]
        return acc.at[k, pl.ds(TILES[k].index(cell) * OWN, OWN)]

    def set_sums(k, first, count):
        labels = jnp.concatenate([wanted[k]] * (count // 128), axis=1)
        rows = pl.ds(first, count)
        sets = set_ref[:, rows].astype(jnp.int16)
        member = jnp.where(labels == sets, BF16(1), BF16(0))
        return lax.dot_general(member, values[:, rows], NT, preferred_element_type=F32)

    def early_sums(k, j):
        part = set_sums(k, sum(CHUNKS[:j]), CHUNKS[j])
        acc[k] = part if j == 0 else acc[k] + part

    for j, rows in enumerate(pieces):
        loads[j].wait()
        code = codes[rows, :].astype(F32).astype(BF16).T.astype(F32)
        scale = scales_ref[:, rows]
        scale = jnp.concatenate(
            [jnp.broadcast_to(scale[b : b + 1], (buckets // blocks, CHUNKS[j])) for b in range(blocks)],
            axis=0,
        )
        raw = jnp.dot(live, (code * scale).astype(BF16), preferred_element_type=F32)
        floored = jnp.maximum(raw - strike_ref[:, rows], 0.0)
        values[:, rows] = jnp.where(kind_ref[:, rows] == 1, floored, raw).astype(BF16)
        if j == 0:
            for load in small[4:]:
                load.wait()
        else:
            for k in range(EARLY):
                early_sums(k, j - 1)

    def pair_copy(k):
        return pltpu.make_async_remote_copy(
            src_ref=acc.at[k, pl.ds(TILE // 2, TILE // 2)], dst_ref=pair_in.at[k],
            send_sem=pair_s.at[k], recv_sem=pair_r.at[k],
            device_id={"prod": sibling}, device_id_type=MESH,
        )

    def y_copy(dy, plane):
        return pltpu.make_async_remote_copy(
            src_ref=rows_of((dy, plane)), dst_ref=y_in.at[plane, dy - 1],
            send_sem=y_s.at[plane], recv_sem=y_r.at[plane],
            device_id={"prod": place(z, rows_y[dy], core)}, device_id_type=MESH,
        )

    def y_all(plane):
        return pltpu.make_async_remote_copy(
            src_ref=y_in.at[plane], dst_ref=y_in.at[plane],
            send_sem=y_s.at[plane], recv_sem=y_r.at[plane],
            device_id={"prod": sibling}, device_id_type=MESH,
        )

    def z_copy(plane):
        return pltpu.make_async_remote_copy(
            src_ref=z_out.at[plane], dst_ref=z_in.at[z], send_sem=z_s.at[0], recv_sem=z_r.at[0],
            device_id={"prod": place(planes[plane], y, core)}, device_id_type=MESH,
        )

    def z_all():
        return pltpu.make_async_remote_copy(
            src_ref=z_out, dst_ref=z_in.at[pl.ds(0, Z - 1)], send_sem=z_s.at[0], recv_sem=z_r.at[0],
            device_id={"prod": sibling}, device_id_type=MESH,
        )

    has_next = x < x_size - 1

    def add_pair(k):
        pair_copy(k).wait_recv()
        acc[k, : TILE // 2] += pair_in[k]

    def send_cells(k):
        for dy, plane in sorted(TILES[k], key=lambda cell: cell[0] != 2):
            if dy:
                y_copy(dy, plane).start()

    def y_total(plane):
        y_all(plane).wait_recv()
        return rows_of((0, plane))[...] + y_in[plane, 0] + y_in[plane, 1] + y_in[plane, 2]

    def after_y(plane):
        z_out[plane] = y_total(plane)
        z_copy(plane).start()

    last = len(CHUNKS) - 1
    for k in range(EARLY):
        early_sums(k, last)
        if k == 0:
            pl.semaphore_wait(barrier, len(near) + 1 + has_next.astype(jnp.int32))
        pair_copy(k).start()

    def step(k, carry):
        acc[k] = set_sums(k, 0, trades)
        pair_copy(k).start()

        @pl.when(k == EARLY)
        def _():
            for i in range(EARLY - 1):
                add_pair(i)
                send_cells(i)

        add_pair(k - 1)
        for i in range(EARLY - 1, len(TILES) - 1):
            pl.when(k == i + 1)(functools.partial(send_cells, i))
        for plane in range(len(TILES) - Y_LAG):
            pl.when(k == plane + Y_LAG)(functools.partial(after_y, plane))
        return carry

    lax.fori_loop(EARLY, len(TILES), step, 0)
    after_y(len(TILES) - Y_LAG)
    add_pair(len(TILES) - 1)
    for plane in range(len(TILES) - Y_LAG + 1, OWN_Z):
        after_y(plane)
    diagonal = lax.broadcasted_iota(jnp.int32, (owned, owned), 0) == lax.broadcasted_iota(
        jnp.int32, (owned, owned), 1
    )
    lag = jnp.sum(jnp.where(diagonal, lag_ref[...].astype(F32), 0.0), axis=1, keepdims=True)
    limit = jnp.sum(jnp.where(diagonal, limit_ref[...], 0.0), axis=1, keepdims=True)
    for k in range(len(TILES)):
        pair_copy(k).wait_send()
        y_all(k).wait_send()
    total = y_total(OWN_Z)
    z_all().wait_send()
    z_all().wait_recv()
    z_in[z] = total
    total = z_in[0]
    for j in range(1, Z):
        total = total + z_in[j]

    lag_out[...] = total[:, half:]
    lag_copy = pltpu.make_async_remote_copy(
        src_ref=lag_out, dst_ref=lag_in, send_sem=lag_s.at[0], recv_sem=lag_r.at[0],
        device_id={"date": x_next}, device_id_type=MESH,
    )
    pl.when(has_next)(lag_copy.start)
    pl.when(x > 0)(lag_copy.wait_recv)
    previous = jnp.where(x > 0, lag_in[...], 0.0)
    lag_one = jnp.concatenate([previous[:, paths:], total[:, : 3 * paths]], axis=1)
    lag_two = jnp.concatenate([previous, total[:, : 2 * paths]], axis=1)
    lagged = jnp.where(lag == 1.0, lag_one, jnp.where(lag == 2.0, lag_two, 0.0))
    collateral = jnp.maximum(lagged - limit, 0.0) - jnp.maximum(-lagged - limit, 0.0)
    exposure = jnp.maximum(total - collateral, 0.0)
    for d in range(dates):
        out_ref[d] = exposure[:, d * paths : (d + 1) * paths]

    pl.when(has_next)(lag_copy.wait_send)


def on_device(cash_codes, block_scales, trade_kind, strike, set_of_trade, discount, lag, limit):
    trades, buckets = cash_codes.shape
    dates, _, paths = discount.shape
    columns = dates * paths
    owned = lag.shape[0]
    live = jnp.swapaxes(discount, 1, 2).reshape(columns, buckets)
    vmem, dma = pltpu.VMEM, pltpu.SemaphoreType.DMA
    operands = (
        cash_codes, block_scales.T, trade_kind[None], strike[None], set_of_trade[None], live,
        lag[None], limit[None],
    )
    return pl.pallas_call(
        kernel,
        out_shape=vmem((dates, owned, paths), F32),
        in_specs=[pl.BlockSpec(memory_space=pl.ANY)] * len(operands),
        out_specs=pl.BlockSpec(memory_space=vmem),
        scratch_shapes=[vmem(operand.shape, operand.dtype) for operand in operands]
        + [
            vmem((columns, trades), BF16),
            vmem((len(TILES), TILE, 128), jnp.int16),
            vmem((Z, TILE, columns), F32),
            vmem((Z, TILE // 2, columns), F32),
            vmem((Z, Y - 1, OWN, columns), F32),
            vmem((Z - 1, OWN, columns), F32),
            vmem((Z, OWN, columns), F32),
            vmem((OWN, columns // 2), F32),
            vmem((OWN, columns // 2), F32),
            dma((len(CHUNKS),)), dma((len(operands) - 1,)),
            dma((Z,)), dma((Z,)), dma((Z,)), dma((Z,)),
            dma((1,)), dma((1,)), dma((1,)), dma((1,)),
        ],
        compiler_params=pltpu.CompilerParams(
            collective_id=0, has_side_effects=True, vmem_limit_bytes=63 << 20
        ),
        name="exposure",
    )(*operands)


def solution(mesh):
    placed = (
        P("prod", None), P("prod", None), P("prod"), P("prod"), P("prod"),
        P("date", None, None), P("prod"), P("prod"),
    )
    return jax.shard_map(
        on_device, mesh=mesh, in_specs=placed, out_specs=P("date", "prod", None), check_vma=False
    )
```

time: 31 us -> 29.2 us (0.942)
  Pallas kernels: 29.1 us -> 28 us
  local copies, waits for them, and re-layouts: 1.47 us -> 0.63 us
    pallas_call x1, Pallas kernels: 29.1 us -> 28 us  [on_device(): pl.pallas_call(kernel, out_shape=vmem((dates, owned, paths), F32), in_spe...]
    unnamed x1, local copies, waits for them, and re-layouts: 1.47 us -> 0.63 us
where the time goes in v3:
time: 29.2 us; the launch traced here: 28.7 us
  Pallas kernels  28 us (96%)
  local copies, waits for them, and re-layouts  0.63 us (2%)
    pallas_call x1, Pallas kernels, on_device(): pl.pallas_call(kernel, out_shape=vmem((dates, owned, paths), F32), in_spe...  28 us
    unnamed x1, local copies, waits for them, and re-layouts  0.63 us

profile of v3, /device:TPU:102, one launch (start us, length us, event | category | flops | bytes accessed | tf_op | source)
XLA Modules:
  0.0 28.7 jit_solution(5888642196110633914)
XLA Ops:
  0.0 28.0 %exposure.1 = f32[4,32,64]{2,1,0:T(8,128)S(1)} custom-call(s32[8192,128]{1,0:T(8,128)} %codes_hbm.1, f32[4,8192]{1,0:T(4,128)} %bitcast.9, s32[1,8192]{1,0:T(1,128)} %bitcast.11, f32[1,8192]{1,0:T(1,128)} %bitcast.12, s32[1,8192]{1,0:T(1,128)} %bitcast.13, bf16[256,128]{1,0:T(8,128)(2,1)} %bitcast.10, s32[1,32]{1,0:T(1,128)} %bitcast.14, f32[1,32]{1,0:T(1,128)} %bitcast.15), custom_call_target="tpu_custom_call" | custom-call | tf_op jit(solution)/shard_map/exposure/pallas_call | solution.py:270
  28.0 0.6 %copy.10 = f32[4,32,64]{2,1,0:T(8,128)} copy(f32[4,32,64]{2,1,0:T(8,128)S(1)} %exposure.1) | data formatting | bytes 65536

commit v4 on v3

--- a/solution.py
+++ b/solution.py
@@ -180,7 +180,7 @@
         acc[k, : TILE // 2] += pair_in[k]
 
     def send_cells(k):
-        for dy, plane in sorted(TILES[k], key=lambda cell: cell[0] != 2):
+        for dy, plane in TILES[k]:
             if dy:
                 y_copy(dy, plane).start()
 

time: 29.2 us -> 29.1 us (level); the launches traced: 28.7 us -> 29 us
  Pallas kernels: 28 us -> 28.4 us
    pallas_call x1, Pallas kernels: 28 us -> 28.4 us  [on_device(): pl.pallas_call(kernel, out_shape=vmem((dates, owned, paths), F32), in_spe...]
where the time goes in v4:
time: 29.1 us; the launch traced here: 29 us
  Pallas kernels  28.4 us (98%)
  local copies, waits for them, and re-layouts  0.63 us (2%)
    pallas_call x1, Pallas kernels, on_device(): pl.pallas_call(kernel, out_shape=vmem((dates, owned, paths), F32), in_spe...  28.4 us
    unnamed x1, local copies, waits for them, and re-layouts  0.63 us

profile of v4, /device:TPU:102, one launch (start us, length us, event | category | flops | bytes accessed | tf_op | source)
XLA Modules:
  0.0 29.0 jit_solution(10741330599055800201)
XLA Ops:
  0.0 28.4 %exposure.1 = f32[4,32,64]{2,1,0:T(8,128)S(1)} custom-call(s32[8192,128]{1,0:T(8,128)} %codes_hbm.1, f32[4,8192]{1,0:T(4,128)} %bitcast.9, s32[1,8192]{1,0:T(1,128)} %bitcast.11, f32[1,8192]{1,0:T(1,128)} %bitcast.12, s32[1,8192]{1,0:T(1,128)} %bitcast.13, bf16[256,128]{1,0:T(8,128)(2,1)} %bitcast.10, s32[1,32]{1,0:T(1,128)} %bitcast.14, f32[1,32]{1,0:T(1,128)} %bitcast.15), custom_call_target="tpu_custom_call" | custom-call | tf_op jit(solution)/shard_map/exposure/pallas_call | solution.py:270
  28.4 0.6 %copy.10 = f32[4,32,64]{2,1,0:T(8,128)} copy(f32[4,32,64]{2,1,0:T(8,128)S(1)} %exposure.1) | data formatting | bytes 65536

commit v5 on v4

--- a/solution.py
+++ b/solution.py
@@ -24,7 +24,7 @@
     ((3, 6), (1, 7), (2, 7), (3, 7)),
     ((0, 4), (0, 5), (0, 6), (0, 7)),
 )
-CHUNKS = (2048, 2048, 2048, 2048)
+CHUNKS = (1024, 1024, 2048, 2048, 2048)
 Y_LAG = 5
 EARLY = 2
 F32, BF16 = jnp.float32, jnp.bfloat16
@@ -123,7 +123,11 @@
         acc[k] = part if j == 0 else acc[k] + part
 
     for j, rows in enumerate(pieces):
-        loads[j].wait()
+        if j < 2:
+            loads[j].wait()
+        elif j == 2:
+            for load in loads[2:]:
+                load.wait()
         code = codes[rows, :].astype(F32).astype(BF16).T.astype(F32)
         scale = scales_ref[:, rows]
         scale = jnp.concatenate(
@@ -212,12 +216,13 @@
         add_pair(k - 1)
         for i in range(EARLY - 1, len(TILES) - 1):
             pl.when(k == i + 1)(functools.partial(send_cells, i))
-        for plane in range(len(TILES) - Y_LAG):
-            pl.when(k == plane + Y_LAG)(functools.partial(after_y, plane))
+        pl.when(k == 5)(functools.partial(after_y, 0))
+        pl.when(k == 6)(functools.partial(after_y, 1))
         return carry
 
     lax.fori_loop(EARLY, len(TILES), step, 0)
-    after_y(len(TILES) - Y_LAG)
+    after_y(2)
+    after_y(3)
     add_pair(len(TILES) - 1)
     for plane in range(len(TILES) - Y_LAG + 1, OWN_Z):
         after_y(plane)
@@ -226,23 +231,22 @@
     )
     lag = jnp.sum(jnp.where(diagonal, lag_ref[...].astype(F32), 0.0), axis=1, keepdims=True)
     limit = jnp.sum(jnp.where(diagonal, limit_ref[...], 0.0), axis=1, keepdims=True)
-    for k in range(len(TILES)):
-        pair_copy(k).wait_send()
-        y_all(k).wait_send()
     total = y_total(OWN_Z)
-    z_all().wait_send()
     z_all().wait_recv()
     z_in[z] = total
+    ahead = z_in[0, :, half:]
+    for j in range(1, Z):
+        ahead = ahead + z_in[j, :, half:]
+    lag_out[...] = ahead
+
+    lag_copy = pltpu.make_async_remote_copy(
+        src_ref=lag_out, dst_ref=lag_in, send_sem=lag_s.at[0], recv_sem=lag_r.at[0],
+        device_id={"date": x_next}, device_id_type=MESH,
+    )
+    pl.when(has_next)(lag_copy.start)
     total = z_in[0]
     for j in range(1, Z):
         total = total + z_in[j]
-
-    lag_out[...] = total[:, half:]
-    lag_copy = pltpu.make_async_remote_copy(
-        src_ref=lag_out, dst_ref=lag_in, send_sem=lag_s.at[0], recv_sem=lag_r.at[0],
-        device_id={"date": x_next}, device_id_type=MESH,
-    )
-    pl.when(has_next)(lag_copy.start)
     pl.when(x > 0)(lag_copy.wait_recv)
     previous = jnp.where(x > 0, lag_in[...], 0.0)
     lag_one = jnp.concatenate([previous[:, paths:], total[:, : 3 * paths]], axis=1)
@@ -253,6 +257,10 @@
     for d in range(dates):
         out_ref[d] = exposure[:, d * paths : (d + 1) * paths]
 
+    for k in range(len(TILES)):
+        pair_copy(k).wait_send()
+        y_all(k).wait_send()
+    z_all().wait_send()
     pl.when(has_next)(lag_copy.wait_send)
 
 

time: 29.1 us -> 29.1 us (level)
  no operation moved by 1% of the time
where the time goes in v5:
time: 29.1 us
  Pallas kernels  28.4 us (98%)
  local copies, waits for them, and re-layouts  0.63 us (2%)
    pallas_call x1, Pallas kernels, on_device(): pl.pallas_call(kernel, out_shape=vmem((dates, owned, paths), F32), in_spe...  28.4 us
    unnamed x1, local copies, waits for them, and re-layouts  0.63 us

profile of v5, /device:TPU:102, one launch (start us, length us, event | category | flops | bytes accessed | tf_op | source)
XLA Modules:
  0.0 29.1 jit_solution(9533045564169439667)
XLA Ops:
  0.0 28.4 %exposure.1 = f32[4,32,64]{2,1,0:T(8,128)S(1)} custom-call(s32[8192,128]{1,0:T(8,128)} %codes_hbm.1, f32[4,8192]{1,0:T(4,128)} %bitcast.9, s32[1,8192]{1,0:T(1,128)} %bitcast.11, f32[1,8192]{1,0:T(1,128)} %bitcast.12, s32[1,8192]{1,0:T(1,128)} %bitcast.13, bf16[256,128]{1,0:T(8,128)(2,1)} %bitcast.10, s32[1,32]{1,0:T(1,128)} %bitcast.14, f32[1,32]{1,0:T(1,128)} %bitcast.15), custom_call_target="tpu_custom_call" | custom-call | tf_op jit(solution)/shard_map/exposure/pallas_call | solution.py:278
  28.4 0.6 %copy.10 = f32[4,32,64]{2,1,0:T(8,128)} copy(f32[4,32,64]{2,1,0:T(8,128)S(1)} %exposure.1) | data formatting | bytes 65536

commit v6 on v4

--- a/solution.py
+++ b/solution.py
@@ -212,12 +212,13 @@
         add_pair(k - 1)
         for i in range(EARLY - 1, len(TILES) - 1):
             pl.when(k == i + 1)(functools.partial(send_cells, i))
-        for plane in range(len(TILES) - Y_LAG):
-            pl.when(k == plane + Y_LAG)(functools.partial(after_y, plane))
+        pl.when(k == 6)(functools.partial(after_y, 0))
+        pl.when(k == 6)(functools.partial(after_y, 1))
+        pl.when(k == 7)(functools.partial(after_y, 2))
         return carry
 
     lax.fori_loop(EARLY, len(TILES), step, 0)
-    after_y(len(TILES) - Y_LAG)
+    after_y(3)
     add_pair(len(TILES) - 1)
     for plane in range(len(TILES) - Y_LAG + 1, OWN_Z):
         after_y(plane)

time: 29.1 us -> 29.1 us (level)
  no operation moved by 1% of the time
where the time goes in v6:
time: 29.1 us; the launch traced here: 29 us
  Pallas kernels  28.4 us (98%)
  local copies, waits for them, and re-layouts  0.63 us (2%)
    pallas_call x1, Pallas kernels, on_device(): pl.pallas_call(kernel, out_shape=vmem((dates, owned, paths), F32), in_spe...  28.4 us
    unnamed x1, local copies, waits for them, and re-layouts  0.63 us

profile of v6, /device:TPU:102, one launch (start us, length us, event | category | flops | bytes accessed | tf_op | source)
XLA Modules:
  0.0 29.0 jit_solution(13062704125392970150)
XLA Ops:
  0.0 28.4 %exposure.1 = f32[4,32,64]{2,1,0:T(8,128)S(1)} custom-call(s32[8192,128]{1,0:T(8,128)} %codes_hbm.1, f32[4,8192]{1,0:T(4,128)} %bitcast.9, s32[1,8192]{1,0:T(1,128)} %bitcast.11, f32[1,8192]{1,0:T(1,128)} %bitcast.12, s32[1,8192]{1,0:T(1,128)} %bitcast.13, bf16[256,128]{1,0:T(8,128)(2,1)} %bitcast.10, s32[1,32]{1,0:T(1,128)} %bitcast.14, f32[1,32]{1,0:T(1,128)} %bitcast.15), custom_call_target="tpu_custom_call" | custom-call | tf_op jit(solution)/shard_map/exposure/pallas_call | solution.py:271
  28.4 0.6 %copy.10 = f32[4,32,64]{2,1,0:T(8,128)} copy(f32[4,32,64]{2,1,0:T(8,128)S(1)} %exposure.1) | data formatting | bytes 65536
